TPU v7x, 128 devices: a whole 4x4x4 slice. The times are simulated.
128 devices in a mesh: grp: 8 (over y, core), dev: 16 (over z, x).
Axes of the slice: x: 4, y: 4, z: 4, core: 2. Of those that a mesh axis runs over, the one named last changes fastest.
Arguments:
- blocks: float32 [32768, 128, 128], P(('grp', 'dev')), may hold values from -0.0625 to 0.0625
- panel: float32 [262144, 64], P(('grp', 'dev')), may hold values from -6 to 6
- block_rows: int32 [32768], P(('grp', 'dev')), may hold values from 0 to 511, as said below
- block_cols: int32 [32768], P(('grp', 'dev')), may hold values from 0 to 15
Outputs:
- basis: float32 [65536, 64], P(('grp', 'dev'))
- r_factor: float32 [64, 64], replicated
Inputs may be any that keep to these rules, and one draw needn't show every extreme that they name: The blocks held by one device are distinct (block_rows, block_cols) pairs. Block row i belongs to device i // 4; among the blocks of one device at most 2 distinct block rows belong to any one device, and in every draw some device's blocks reach 2 distinct block rows of one device.
All inputs are finite; a program needn't handle non-finite values.
Results may differ from a plain program's by a relative error of at most 0.0001.
Values sent between devices are 32-bit elements; how exact they have to be, the bound alone decides.
A program may use at most 128 MiB of HBM per device.

v0:
```python
import jax
import jax.numpy as jnp
from jax import lax
from jax.sharding import PartitionSpec as P

RB_DEV = 4
CAP = 2


def combined_all(array, axis, combine):
    everything = lax.all_gather(array, axis)
    leading = everything[0]

    def step(k, so_far):
        return combine(so_far, everything[k])

    return lax.fori_loop(1, lax.axis_size(axis), step, leading)


def combine_upper(left, right):
    gram = jnp.dot(left.T, left, precision=lax.Precision.HIGHEST) + jnp.dot(
        right.T, right, precision=lax.Precision.HIGHEST
    )
    return jnp.linalg.cholesky(gram).T


def per_device(blocks, panel, block_rows, block_cols):
    dest_count = lax.axis_size(("grp", "dev"))
    block_size = blocks.shape[1]
    rank_cols = panel.shape[1]
    rows_owned = RB_DEV
    slot_count = CAP
    total_blocks = dest_count * rows_owned
    total_rows = total_blocks * block_size
    chosen = panel.reshape(-1, block_size, rank_cols)[block_cols]
    partial_sum = jnp.einsum("bij,bjr->bir", blocks, chosen, precision=lax.Precision.HIGHEST)
    onehot = block_rows[:, None] == jnp.arange(total_blocks, dtype=jnp.int32)[None, :]
    present = jnp.any(onehot, axis=0).reshape(dest_count, rows_owned)
    slot_grid = jnp.cumsum(present.astype(jnp.int32), axis=1) - 1
    block_slot = jnp.sum(jnp.where(onehot, slot_grid.reshape(-1)[None, :], 0), axis=1)
    target = block_rows // rows_owned * slot_count + block_slot
    outgoing = jax.ops.segment_sum(partial_sum, target, num_segments=dest_count * slot_count)
    outgoing = outgoing.reshape(dest_count, slot_count, block_size, rank_cols)
    match = present[:, :, None] & (
        slot_grid[:, :, None] == jnp.arange(slot_count, dtype=jnp.int32)[None, None, :]
    )
    local_index = jnp.sum(
        jnp.where(match, jnp.arange(rows_owned, dtype=jnp.int32)[None, :, None], 0), axis=1
    )
    filled = jnp.any(match, axis=1)
    slot_rows = jnp.where(filled, local_index, -1).astype(jnp.float32)
    received, received_rows = (
        lax.all_to_all(outgoing, ("grp", "dev"), split_axis=0, concat_axis=0, tiled=True),
        lax.all_to_all(slot_rows, ("grp", "dev"), split_axis=0, concat_axis=0, tiled=True),
    )
    select = (
        received_rows.reshape(-1)[:, None] == jnp.arange(rows_owned, dtype=jnp.float32)[None, :]
    ).astype(jnp.float32)
    local_panel = jnp.einsum(
        "sl,sir->lir",
        select,
        received.reshape(-1, block_size, rank_cols),
        precision=lax.Precision.HIGHEST,
    )
    flat_panel = local_panel.reshape(rows_owned * block_size, rank_cols)
    local_gram = jnp.dot(flat_panel.T, flat_panel, precision=lax.Precision.HIGHEST) / total_rows
    upper = jnp.linalg.cholesky(local_gram).T
    upper = combined_all(upper, "dev", combine_upper)
    upper = combined_all(upper, "grp", combine_upper)
    lower = upper.T
    basis = lax.linalg.triangular_solve(lower, flat_panel.T, left_side=True, lower=True).T
    return (basis, upper)


def solution(mesh):
    placed = (
        P(("grp", "dev"), None, None),
        P(("grp", "dev"), None),
        P(("grp", "dev")),
        P(("grp", "dev")),
    )
    return jax.shard_map(
        per_device,
        mesh=mesh,
        in_specs=placed,
        out_specs=(P(("grp", "dev"), None), P()),
        check_vma=False,
    )
```

profile of v0, /device:TPU:0, one launch (start us, length us, event | category | flops | bytes accessed | tf_op | source)
XLA Modules:
  0.0 464.1 jit_solution(50358718281335226)
XLA Ops:
  2.9 11.1 %all-to-all-start = ((f32[128,1,2]{2,1,0:T(1,128)}), f32[128,1,2]{2,1,0:T(1,128)S(1)}, u32[]{:S(2)}, u32[]{:S(2)}) async-start(f32[128,1,2]{2,1,0:T(1,128)} %copy.75), calls=%async_computation | async-start | bytes 131072 | tf_op jit(solution)/shard_map/all_to_all | solution.py:54
  20.1 36.8 %convolution_bitcast_fusion = f32[256,128,64]{1,2,0:T(8,128)} fusion(f32[256,128,64]{1,2,0:T(8,128)} %gather_fusion, f32[256,128,128]{2,1,0:T(8,128)} %param.9), kind=kOutput, calls=%fused_computation.24 | convolution fusion | flops 3221225472 | bytes 33554432 | tf_op jit(solution)/shard_map/bij,bjr->bir/dot_general | solution.py:36
  61.2 39.3 %scatter_fusion = f32[256,128,64]{1,2,0:T(8,128)} fusion(f32[256,128,64]{1,2,0:T(8,128)} %broadcast_in_dim.47, s32[256]{0:T(256)S(1)} %multiply_add_fusion, f32[256,128,64]{1,2,0:T(8,128)} %convolution_bitcast_fusion), kind=kCustom, calls=%fused_computation.1 | custom fusion | flops 2097152 | bytes 25166848 | tf_op jit(solution)/shard_map/scatter-add | solution.py:42
  100.5 15.3 %copy.77 = f32[128,2,128,64]{2,1,3,0:T(2,128)} copy(f32[128,2,128,64]{2,3,1,0:T(8,128)} %bitcast.86) | data formatting | bytes 16777216 | tf_op jit(solution)/shard_map/reshape | solution.py:43
  115.8 10.6 %all-to-all-start.1 = ((f32[128,2,128,64]{2,1,3,0:T(2,128)}), f32[128,2,128,64]{2,1,3,0:T(2,128)}, u32[]{:S(2)}, u32[]{:S(2)}) async-start(f32[128,2,128,64]{2,1,3,0:T(2,128)} %copy.77), calls=%async_computation.1 | async-start | bytes 16777216 | tf_op jit(solution)/shard_map/all_to_all | solution.py:53
  127.8 98.6 %all-to-all-done.1 = f32[128,2,128,64]{2,1,3,0:T(2,128)} async-done(((f32[128,2,128,64]{2,1,3,0:T(2,128)}), f32[128,2,128,64]{2,1,3,0:T(2,128)}, u32[]{:S(2)}, u32[]{:S(2)}) %all-to-all-start.1) | async-done | bytes 8388640 | tf_op jit(solution)/shard_map/all_to_all | solution.py:53
  242.6 28.2 %all-gather = f32[1024,64]{1,0:T(8,128)S(1)} all-gather(f32[64,64]{1,0:T(8,128)S(1)} %copy.83), channel_id=2, replica_groups=mesh['grp'=8,'dev'=16] {'dev'}, dimensions={0}, use_global_device_ids=true | all-gather | bytes 278528 | tf_op jit(solution)/shard_map/all_gather | solution.py:11
  270.9 116.1 %while.30 = (s32[]{:T(128)}, f32[64,64]{0,1:T(8,128)S(1)}, f32[16,64,64]{2,1,0:T(8,128)S(1)}, s32[]{:T(128)}, s32[]{:T(128)}, /*index=5*/s32[]{:T(128)}) while((s32[]{:T(128)}, f32[64,64]{0,1:T(8,128)S(1)}, f32[16,64,64]{2,1,0:T(8,128)S(1)}, s32[]{:T(128)}, s32[]{:T(128)}, /*index=5*/s32[]{:T(128)}) %tuple.90), condition=%wide.region_9.11_spmd, body=%wide.region_8.10_spmd.sunk | while | flops 6328388 | bytes 246389 | solution.py:17
  286.9 5.8 %cholesky.171 = f32[64,64]{1,0:T(8,128)S(1)} custom-call(f32[64,64]{1,0:T(8,128)S(1)} %fusion.47), custom_call_target="Cholesky" | custom-call | tf_op jit(solution)/shard_map/while/body/eval_jaxpr/jit(cholesky)/cholesky | solution.py:24
  294.6 5.8 %cholesky.171 = f32[64,64]{1,0:T(8,128)S(1)} custom-call(f32[64,64]{1,0:T(8,128)S(1)} %fusion.47), custom_call_target="Cholesky" | custom-call | tf_op jit(solution)/shard_map/while/body/eval_jaxpr/jit(cholesky)/cholesky | solution.py:24
  302.4 5.8 %cholesky.171 = f32[64,64]{1,0:T(8,128)S(1)} custom-call(f32[64,64]{1,0:T(8,128)S(1)} %fusion.47), custom_call_target="Cholesky" | custom-call | tf_op jit(solution)/shard_map/while/body/eval_jaxpr/jit(cholesky)/cholesky | solution.py:24
  310.1 5.8 %cholesky.171 = f32[64,64]{1,0:T(8,128)S(1)} custom-call(f32[64,64]{1,0:T(8,128)S(1)} %fusion.47), custom_call_target="Cholesky" | custom-call | tf_op jit(solution)/shard_map/while/body/eval_jaxpr/jit(cholesky)/cholesky | solution.py:24
  317.9 5.8 %cholesky.171 = f32[64,64]{1,0:T(8,128)S(1)} custom-call(f32[64,64]{1,0:T(8,128)S(1)} %fusion.47), custom_call_target="Cholesky" | custom-call | tf_op jit(solution)/shard_map/while/body/eval_jaxpr/jit(cholesky)/cholesky | solution.py:24
  325.6 5.8 %cholesky.171 = f32[64,64]{1,0:T(8,128)S(1)} custom-call(f32[64,64]{1,0:T(8,128)S(1)} %fusion.47), custom_call_target="Cholesky" | custom-call | tf_op jit(solution)/shard_map/while/body/eval_jaxpr/jit(cholesky)/cholesky | solution.py:24
  333.4 5.8 %cholesky.171 = f32[64,64]{1,0:T(8,128)S(1)} custom-call(f32[64,64]{1,0:T(8,128)S(1)} %fusion.47), custom_call_target="Cholesky" | custom-call | tf_op jit(solution)/shard_map/while/body/eval_jaxpr/jit(cholesky)/cholesky | solution.py:24
  341.1 5.8 %cholesky.171 = f32[64,64]{1,0:T(8,128)S(1)} custom-call(f32[64,64]{1,0:T(8,128)S(1)} %fusion.47), custom_call_target="Cholesky" | custom-call | tf_op jit(solution)/shard_map/while/body/eval_jaxpr/jit(cholesky)/cholesky | solution.py:24
  348.8 5.8 %cholesky.171 = f32[64,64]{1,0:T(8,128)S(1)} custom-call(f32[64,64]{1,0:T(8,128)S(1)} %fusion.47), custom_call_target="Cholesky" | custom-call | tf_op jit(solution)/shard_map/while/body/eval_jaxpr/jit(cholesky)/cholesky | solution.py:24
  356.6 5.8 %cholesky.171 = f32[64,64]{1,0:T(8,128)S(1)} custom-call(f32[64,64]{1,0:T(8,128)S(1)} %fusion.47), custom_call_target="Cholesky" | custom-call | tf_op jit(solution)/shard_map/while/body/eval_jaxpr/jit(cholesky)/cholesky | solution.py:24
  364.3 5.8 %cholesky.171 = f32[64,64]{1,0:T(8,128)S(1)} custom-call(f32[64,64]{1,0:T(8,128)S(1)} %fusion.47), custom_call_target="Cholesky" | custom-call | tf_op jit(solution)/shard_map/while/body/eval_jaxpr/jit(cholesky)/cholesky | solution.py:24
  372.1 5.8 %cholesky.171 = f32[64,64]{1,0:T(8,128)S(1)} custom-call(f32[64,64]{1,0:T(8,128)S(1)} %fusion.47), custom_call_target="Cholesky" | custom-call | tf_op jit(solution)/shard_map/while/body/eval_jaxpr/jit(cholesky)/cholesky | solution.py:24
  379.8 5.8 %cholesky.171 = f32[64,64]{1,0:T(8,128)S(1)} custom-call(f32[64,64]{1,0:T(8,128)S(1)} %fusion.47), custom_call_target="Cholesky" | custom-call | tf_op jit(solution)/shard_map/while/body/eval_jaxpr/jit(cholesky)/cholesky | solution.py:24
  387.1 16.1 %all-gather.1 = f32[512,64]{1,0:T(8,128)S(1)} all-gather(f32[64,64]{1,0:T(8,128)S(1)} %copy.85), channel_id=3, replica_groups=mesh['grp'=8,'dev'=16] {'grp'}, dimensions={0}, use_global_device_ids=true | all-gather | bytes 147456 | tf_op jit(solution)/shard_map/all_gather | solution.py:11
  403.3 54.2 %while.31 = (s32[]{:T(128)}, f32[64,64]{0,1:T(8,128)S(1)}, f32[8,64,64]{2,1,0:T(8,128)S(1)}, s32[]{:T(128)}, s32[]{:T(128)}, /*index=5*/s32[]{:T(128)}) while((s32[]{:T(128)}, f32[64,64]{0,1:T(8,128)S(1)}, f32[8,64,64]{2,1,0:T(8,128)S(1)}, s32[]{:T(128)}, s32[]{:T(128)}, /*index=5*/s32[]{:T(128)}) %tuple.91), condition=%wide.region_11.13_spmd, body=%wide.region_10.12_spmd.sunk | while | flops 6328388 | bytes 246389 | solution.py:17
  403.8 5.8 %cholesky.183 = f32[64,64]{1,0:T(8,128)S(1)} custom-call(f32[64,64]{1,0:T(8,128)S(1)} %fusion.52), custom_call_target="Cholesky" | custom-call | tf_op jit(solution)/shard_map/while/body/eval_jaxpr/jit(cholesky)/cholesky | solution.py:24
  (210 shorter events, 124.1 us)
Async XLA Ops:
  0.6 14.4 %copy-start = (f32[2048,64]{0,1:T(8,128)S(1)}, f32[2048,64]{0,1:T(8,128)}, u32[]{:S(2)}) copy-start(f32[2048,64]{0,1:T(8,128)} %param.10) | copy-start | bytes 1572868
  2.9 112.9 %all-to-all-start = ((f32[128,1,2]{2,1,0:T(1,128)}), f32[128,1,2]{2,1,0:T(1,128)S(1)}, u32[]{:S(2)}, u32[]{:S(2)}) async-start(f32[128,1,2]{2,1,0:T(1,128)} %copy.75), calls=%async_computation | async-start | bytes 131072 | tf_op jit(solution)/shard_map/all_to_all | solution.py:54
  20.1 36.8 %copy-start.2 = (s32[256]{0:T(256)S(1)}, s32[256]{0:T(256)}, u32[]{:S(2)}) copy-start(s32[256]{0:T(256)} %param.11) | copy-start | bytes 3076
  115.8 110.7 %all-to-all-start.1 = ((f32[128,2,128,64]{2,1,3,0:T(2,128)}), f32[128,2,128,64]{2,1,3,0:T(2,128)}, u32[]{:S(2)}, u32[]{:S(2)}) async-start(f32[128,2,128,64]{2,1,3,0:T(2,128)} %copy.77), calls=%async_computation.1 | async-start | bytes 16777216 | tf_op jit(solution)/shard_map/all_to_all | solution.py:53
  226.5 237.6 %copy-start.1 = (f32[2048,64]{0,1:T(8,128)S(1)}, f32[2048,64]{0,1:T(8,128)}, u32[]{:S(2)}) copy-start(f32[2048,64]{0,1:T(8,128)} %param.10) | copy-start | bytes 1572868
where the time goes:
time: 466 us; the launch traced here: 464 us
  other arithmetic  213 us (46%)
  waiting for transfers between devices  98.6 us (21%)
  matrix products  50.4 us (11%)
  blocking collectives  44.3 us (10%)
  local copies, waits for them, and re-layouts  34 us (7%)
  starting transfers between devices  21.7 us (5%)
    another operation x66, other arithmetic, combine_upper(): return jnp.linalg.cholesky(gram).T  143 us
    all_to_all x1, waiting for transfers between devices, per_device(): lax.all_to_all(outgoing, ('grp', 'dev'), split_axis=0, concat_axis=0, til...  98.6 us
    all_gather x2, blocking collectives, combined_all(): everything = lax.all_gather(array, axis)  44.3 us
    scatter-add x1, other arithmetic, per_device(): jax.ops.segment_sum(partial_sum, target, num_segments=dest_count * slot_c...  39.3 us
    dot_general x1, matrix products, per_device(): jnp.einsum('bij,bjr->bir', blocks, chosen, precision=lax.Precision.HIGHEST)  36.8 us
    reshape x1, local copies, waits for them, and re-layouts, per_device(): outgoing = outgoing.reshape(dest_count, slot_count, block_size, rank_cols)  15.3 us
    transpose x22, other arithmetic, combine_upper(): return jnp.linalg.cholesky(gram).T  14.3 us
    all_to_all x1, starting transfers between devices, per_device(): lax.all_to_all(slot_rows, ('grp', 'dev'), split_axis=0, concat_axis=0, ti...  11.1 us
  transfers between devices with their start and end apart: 2, of which 1 were waited for; matrix products, arithmetic and copies ran while one was open for 22% of the time, Pallas kernels for 0%

commit v1 on v0

v1 whole, which is shorter than its diff:
```python
import functools

import jax
import jax.numpy as jnp
from jax import lax
from jax.experimental import pallas as pl
from jax.experimental.pallas import tpu as pltpu
from jax.sharding import PartitionSpec as P

MESH = pl.DeviceIdType.MESH
F32 = jnp.float32
BF16 = jnp.bfloat16
NB = 256
BS = 128
RANK = 64
ROWS = 4
NRB = 512
HALF = BS // 2
PK = HALF // 2
CHUNKS = 8
PER = NB // CHUNKS
GROUP = 8
AXES = ("x", "y", "z")
STRIDE = {"x": 1, "z": 4, "y": 32}
FLOWS = (
    (0, 0, 6, "xyz"),
    (0, 6, 11, "yzx"),
    (0, 11, 16, "zxy"),
    (1, 0, 5, "xyz"),
    (1, 5, 11, "yzx"),
    (1, 11, 16, "zxy"),
)
NF = len(FLOWS)
ORDER = (2, 3, 1, 0)


def coords():
    g, d = lax.axis_index("grp"), lax.axis_index("dev")
    return {"x": d % 4, "z": d // 4, "y": g // 2, "c": g % 2}


def device(me, **moved):
    at = dict(me)
    at.update(moved)
    return (at["y"] * 2 + at["c"], at["z"] * 4 + at["x"])


def neighbour(me, axis, step):
    return device(me, **{axis: (me[axis] + step + 4) % 4})


def groups_of(first, end):
    out, tile = [], first
    while tile < end:
        row, within = divmod(tile, 4)
        count = min(4 - within, end - tile)
        out.append((row, within, count, tile - first))
        tile += count
    return out


def remote(src, dst, send, recv, to):
    return pltpu.make_async_remote_copy(
        src_ref=src, dst_ref=dst, send_sem=send, recv_sem=recv, device_id=to, device_id_type=MESH
    )


def reduce_kernel(*refs):
    meta, panel, blocks, prod_ref, gram_ref = refs[:5]
    refs = list(refs[5:])
    held, weights, sums = refs[:3]
    refs = refs[3:]
    mine_out, pair_in, a1, b1, b2, s1, a2, b12, b22, q2, c3 = (
        refs[NF * i : NF * (i + 1)] for i in range(11)
    )
    (gbuf, hbm_sem, pair_s, pair_r, one_s, one_r, two_s, two_r, three_s, three_r, gram_s, gram_r) = refs[NF * 11 :]
    me = coords()

    loads = []
    for half in range(2):
        for c in range(CHUNKS):
            part = (pl.ds(c * PER, PER), pl.ds(half * HALF, HALF))
            copy = pltpu.make_async_copy(blocks.at[part], held.at[part], hbm_sem.at[half, c])
            copy.start()
            loads.append(copy)

    barrier = pltpu.get_barrier_semaphore()
    peers = [device(me, c=1 - me["c"])]
    for axis in AXES:
        peers += [neighbour(me, axis, step) for step in (1, 2, 3)]
    for peer in peers:
        pl.semaphore_signal(barrier, inc=1, device_id=peer, device_id_type=MESH)

    lane_low = lax.broadcasted_iota(jnp.int32, (PK, BS), 1) < RANK

    def prepare(c, _):
        p = panel[pl.ds(pl.multiple_of(c * BS, BS), BS), :]
        high = p.astype(BF16)
        low = (p - high.astype(F32)).astype(BF16)
        both = jnp.concatenate([high, low], axis=1)
        weights[c, :BS, :] = both
        weights[c, BS:, :] = both
        return 0

    lax.fori_loop(0, 16, prepare, 0)
    for half in range(2):
        sums[half, NB] = jnp.zeros((PK, BS), F32)

    def multiply(half, c):
        loads[half * CHUNKS + c].wait()

        def step(g, _):
            base = c * PER + g * GROUP
            out = []
            for i in range(GROUP):
                k = base + i
                x = held[k, half * HALF : (half + 1) * HALF, :]
                high = x.astype(BF16)
                low = (x - high.astype(F32)).astype(BF16)
                left = jnp.concatenate([high, low], axis=1)
                u = jnp.dot(left, weights[meta[k]], preferred_element_type=F32)
                top, bottom = u[:PK], u[PK:]
                out.append(
                    jnp.where(lane_low, top, bottom)
                    + pltpu.roll(jnp.where(lane_low, bottom, top), RANK, 1)
                )
            for i in range(GROUP):
                k = base + i
                sums[half, k] = out[i] + sums[half, meta[NB + k]]
            return 0

        lax.fori_loop(0, PER // GROUP, step, 0)

    def owner(f, core, ua, ub, uc):
        half, _, _, order = FLOWS[f]
        sign = 1 if half == 0 else -1
        at = core * 16
        for axis, u in zip(order, (ua, ub, uc)):
            at = at + STRIDE[axis] * ((me[axis] + (sign * u) % 4) % 4)
        return at

    def own_rows(f, core, ua, ub, uc):
        half, first, end, _ = FLOWS[f]
        o = owner(f, core, ua, ub, uc)
        for row, within, count, offset in groups_of(first, end):
            at = meta[2 * NB + o * ROWS + row]
            yield offset, count, sums[half, at, within * 8 : (within + count) * 8, :]

    def neigh(f, order_at, direction):
        half, _, _, order = FLOWS[f]
        sign = 1 if half == 0 else -1
        return neighbour(me, order[order_at], sign * direction)

    started = []

    def go(copy):
        copy.start()
        started.append(copy)
        return copy

    def pair_copy(f, ua):
        return remote(
            mine_out[f].at[ua], pair_in[f].at[ua], pair_s.at[f, ua], pair_r.at[f, ua], device(me, c=1 - me["c"])
        )

    def fill(f, ua):
        for ub in range(4):
            for uc in range(4):
                for offset, count, value in own_rows(f, 1 - me["c"], ua, ub, uc):
                    mine_out[f][ua, ub, uc, offset * 8 : (offset + count) * 8, :] = value
        return go(pair_copy(f, ua))

    def one_copy(f, kind, ub):
        ua, buf, direction = ((2, a1, 1), (3, b1, -1), (1, b2, 1))[kind]
        return remote(
            pair_in[f].at[ua, ub], buf[f].at[ub], one_s.at[f, kind, ub], one_r.at[f, kind, ub], neigh(f, 0, direction)
        )

    def chip_sum(f, ua, ub, extra, out):
        for uc in range(4):
            for offset, count, value in own_rows(f, me["c"], ua, ub, uc):
                rows = slice(offset * 8, (offset + count) * 8)
                value = value + pair_in[f][ua, ub, uc, rows, :]
                for e in extra:
                    value = value + e[f][ub, uc, rows, :]
                out[uc, rows, :] = value

    def begin(flows):
        pairs = {}
        for ua in ORDER:
            for f in flows:
                pairs[f, ua] = fill(f, ua)
        for kind, ua in ((0, 2), (1, 3)):
            for f in flows:
                pairs[f, ua].wait_recv()
                for ub in ORDER:
                    chip_sum(f, ua, ub, (), pair_in[f].at[ua, ub])
                    go(one_copy(f, kind, ub))
        return pairs

    for c in range(CHUNKS):
        multiply(0, c)
    pl.semaphore_wait(barrier, len(peers))
    pairs = begin((0, 1, 2))
    for c in range(CHUNKS):
        multiply(1, c)
    pairs.update(begin((3, 4, 5)))

    for ub in ORDER:
        for f in range(NF):
            if ub == ORDER[0]:
                pairs[f, 1].wait_recv()
            one_copy(f, 0, ub).wait_recv()
            chip_sum(f, 1, ub, (a1,), pair_in[f].at[1, ub])
            go(one_copy(f, 2, ub))

    def two_copy(f, kind):
        ub, buf, direction = ((2, a2, 1), (3, b12, -1), (1, b22, 1))[kind]
        return remote(s1[f].at[ub], buf[f], two_s.at[f, kind], two_r.at[f, kind], neigh(f, 1, direction))

    def three_copy(f, uc):
        return remote(q2[f].at[uc], c3[f].at[uc - 1], three_s.at[f, uc - 1], three_r.at[f, uc - 1], neigh(f, 2, uc))

    for ub in ORDER:
        for f in range(NF):
            if ub == ORDER[0]:
                pairs[f, 0].wait_recv()
            one_copy(f, 1, ub).wait_recv()
            one_copy(f, 2, ub).wait_recv()
            chip_sum(f, 0, ub, (b1, b2), s1[f].at[ub])
            if ub == 2:
                go(two_copy(f, 0))
            elif ub == 3:
                go(two_copy(f, 1))
            elif ub == 1:
                two_copy(f, 0).wait_recv()
                s1[f][1] = s1[f][1] + a2[f][...]
                go(two_copy(f, 2))
    for f in range(NF):
        two_copy(f, 1).wait_recv()
        two_copy(f, 2).wait_recv()
        q2[f][...] = s1[f][0] + b12[f][...] + b22[f][...]
        for uc in (2, 1, 3):
            go(three_copy(f, uc))
    for f in range(NF):
        half, first, end, _ = FLOWS[f]
        for uc in (1, 2, 3):
            three_copy(f, uc).wait_recv()
        prod_ref[half * 128 + first * 8 : half * 128 + end * 8, :] = (
            q2[f][0] + c3[f][0] + (c3[f][1] + c3[f][2])
        )

    prod = prod_ref[...]
    both = lax.dot_general(
        prod, prod, (((0,), (0,)), ((), ())), precision=lax.Precision.HIGHEST, preferred_element_type=F32
    )
    upper, lower = both[:RANK], both[RANK:]
    in_low = upper + pltpu.roll(lower, RANK, 1)
    in_high = pltpu.roll(upper, RANK, 1) + lower
    gbuf[0, 0] = jnp.where(lane_low, in_low[:PK], in_high[PK:]) * (1.0 / (NRB * BS))

    copy = go(remote(gbuf.at[0, 0], gbuf.at[0, 1], gram_s.at[0, 0], gram_r.at[0, 0], device(me, c=1 - me["c"])))
    copy.wait_recv()
    total = gbuf[0, 0] + gbuf[0, 1]
    for i, axis in enumerate(AXES):
        gbuf[i + 1, 0] = total
        copies = [
            go(
                remote(
                    gbuf.at[i + 1, 0],
                    gbuf.at[i + 1, step],
                    gram_s.at[i + 1, step - 1],
                    gram_r.at[i + 1, step - 1],
                    neighbour(me, axis, step),
                )
            )
            for step in (1, 2, 3)
        ]
        for copy in copies:
            copy.wait_recv()
        total = (gbuf[i + 1, 0] + gbuf[i + 1, 2]) + (gbuf[i + 1, 1] + gbuf[i + 1, 3])
    gram_ref[...] = total
    for copy in started:
        copy.wait_send()


def factor_kernel(gram_ref, prod_ref, basis_ref, r_ref):
    lane = lax.broadcasted_iota(jnp.int32, (8, BS), 1)
    sub = lax.broadcasted_iota(jnp.int32, (8, BS), 0)
    packed = gram_ref[...]
    turned = pltpu.roll(packed, RANK, 1)
    tiles = []
    for t in range(8):
        half = packed if t < 4 else turned
        g = half[(t % 4) * 8 : (t % 4 + 1) * 8, :]
        eye = (lane - RANK == sub + t * 8).astype(F32)
        tiles.append(jnp.where(lane < RANK, g, eye))
    diag = [jnp.ones((8, BS), F32)] * 8
    for j in range(RANK):
        tj, jj = divmod(j, 8)
        cols = {t: jnp.broadcast_to(tiles[t][:, j : j + 1], (8, BS)) for t in range(tj, 8)}
        pivot = jnp.broadcast_to(cols[tj][jj : jj + 1, :], (8, BS))
        row = jnp.broadcast_to(tiles[tj][jj : jj + 1, :], (8, BS)) / pivot
        diag[tj] = jnp.where(sub == jj, pivot, diag[tj])
        for t in range(tj, 8):
            col = jnp.where(sub > jj, cols[t], 0.0) if t == tj else cols[t]
            tiles[t] = tiles[t] - col * row
    scaled = jnp.concatenate([tiles[t] / jnp.sqrt(diag[t]) for t in range(8)], axis=0)
    lane = lax.broadcasted_iota(jnp.int32, (RANK, BS), 1)
    sub = lax.broadcasted_iota(jnp.int32, (RANK, BS), 0)
    r_ref[...] = jnp.where(lane >= sub, scaled, 0.0)[:, :RANK]
    inv_high = jnp.where(lane >= RANK, scaled, 0.0)
    inv_low = pltpu.roll(inv_high, RANK, 1)
    prod = prod_ref[...]
    for side, inv in ((0, inv_low), (1, inv_high)):
        out = lax.dot_general(
            prod, inv, (((1,), (1,)), ((), ())), precision=lax.Precision.HIGHEST, preferred_element_type=F32
        )
        for half in range(2):
            for r in range(ROWS):
                to = r * BS + half * HALF + side * PK
                basis_ref[to : to + PK, :] = out[half * BS + r * PK : half * BS + (r + 1) * PK, :]


def reduced(meta, panel, blocks):
    rows = [(end - first) * 8 for _, first, end, _ in FLOWS]

    def per_flow(*lead):
        return [pltpu.VMEM((*lead, n, BS), F32) for n in rows]

    dma = pltpu.SemaphoreType.DMA
    scratch = [
        pltpu.VMEM((NB, BS, BS), F32),
        pltpu.VMEM((16, 2 * BS, BS), BF16),
        pltpu.VMEM((2, NB + 1, PK, BS), F32),
        *per_flow(4, 4, 4),
        *per_flow(4, 4, 4),
        *per_flow(4, 4),
        *per_flow(4, 4),
        *per_flow(4, 4),
        *per_flow(4, 4),
        *per_flow(4),
        *per_flow(4),
        *per_flow(4),
        *per_flow(4),
        *per_flow(3),
        pltpu.VMEM((4, 4, PK, BS), F32),
        dma((2, CHUNKS)),
        dma((NF, 4)),
        dma((NF, 4)),
        dma((NF, 3, 4)),
        dma((NF, 3, 4)),
        dma((NF, 3)),
        dma((NF, 3)),
        dma((NF, 3)),
        dma((NF, 3)),
        dma((4, 3)),
        dma((4, 3)),
    ]
    return pl.pallas_call(
        reduce_kernel,
        out_shape=(jax.ShapeDtypeStruct((256, BS), F32), jax.ShapeDtypeStruct((PK, BS), F32)),
        in_specs=[
            pl.BlockSpec(memory_space=pltpu.SMEM),
            pl.BlockSpec(memory_space=pltpu.VMEM),
            pl.BlockSpec(memory_space=pl.ANY),
        ],
        out_specs=(pl.BlockSpec(memory_space=pltpu.VMEM), pl.BlockSpec(memory_space=pltpu.VMEM)),
        scratch_shapes=scratch,
        compiler_params=pltpu.CompilerParams(collective_id=0, has_side_effects=True, vmem_limit_bytes=60 << 20),
        name="reduce",
    )(meta, panel, blocks)


def factored(gram, prod):
    vmem = pl.BlockSpec(memory_space=pltpu.VMEM)
    return pl.pallas_call(
        factor_kernel,
        out_shape=(jax.ShapeDtypeStruct((512, RANK), F32), jax.ShapeDtypeStruct((RANK, RANK), F32)),
        in_specs=[vmem, vmem],
        out_specs=(vmem, vmem),
        compiler_params=pltpu.CompilerParams(vmem_limit_bytes=16 << 20),
        name="factor",
    )(gram, prod)


def per_device(blocks, panel, block_rows, block_cols):
    k = jnp.arange(NB, dtype=jnp.int32)
    same = (block_rows[:, None] == block_rows[None, :]) & (k[None, :] < k[:, None])
    previous = jnp.max(jnp.where(same, k[None, :], -1), axis=1)
    previous = jnp.where(previous < 0, NB, previous)
    here = block_rows[None, :] == jnp.arange(NRB, dtype=jnp.int32)[:, None]
    last = jnp.max(jnp.where(here, k[None, :], -1), axis=1)
    last = jnp.where(last < 0, NB, last)
    meta = jnp.concatenate([block_cols, previous, last])
    prod, gram = reduced(meta, panel, blocks)
    return factored(gram, prod)


def solution(mesh):
    placed = (
        P(("grp", "dev"), None, None),
        P(("grp", "dev"), None),
        P(("grp", "dev")),
        P(("grp", "dev")),
    )
    return jax.shard_map(
        per_device,
        mesh=mesh,
        in_specs=placed,
        out_specs=(P(("grp", "dev"), None), P()),
        check_vma=False,
    )
```

time: 466 us -> 95.6 us (0.21)
  other arithmetic: 213 us -> 3.05 us
  waiting for transfers between devices: 98.6 us -> 0 us
  Pallas kernels: 0 us -> 86.8 us
  matrix products: 50.4 us -> 0 us
  blocking collectives: 44.3 us -> 0 us
  local copies, waits for them, and re-layouts: 34 us -> 4.76 us
  starting transfers between devices: 21.7 us -> 0 us
    another operation x72 -> x0, other arithmetic: 155 us -> none  [the longest x66 143 us: combine_upper(): return jnp.linalg.cholesky(gram).T]
    all_to_all x2 -> x0, waiting for transfers between devices: 98.6 us -> none  [the longest x1 98.6 us: per_device(): lax.all_to_all(outgoing, ('grp', 'dev'), split_axis=0, concat_axis=0, til...]
    pallas_call x0 -> x2, Pallas kernels: none -> 86.8 us  [the longest x1 77.9 us: reduced(): pl.pallas_call(reduce_kernel, out_shape=(jax.ShapeDtypeStruct((256, BS),...]
    dot_general x47 -> x0, matrix products: 49.4 us -> none  [the longest x1 36.8 us: per_device(): jnp.einsum('bij,bjr->bir', blocks, chosen, precision=lax.Precision.HIGHEST)]
    all_gather x2 -> x0, blocking collectives: 44.3 us -> none  [combined_all(): everything = lax.all_gather(array, axis)]
    scatter-add x1 -> x0, other arithmetic: 39.3 us -> none  [per_device(): jax.ops.segment_sum(partial_sum, target, num_segments=dest_count * slot_c...]
    all_to_all x2 -> x0, starting transfers between devices: 21.7 us -> none  [the longest x1 11.1 us: per_device(): lax.all_to_all(slot_rows, ('grp', 'dev'), split_axis=0, concat_axis=0, ti...]
    reshape x2 -> x0, local copies, waits for them, and re-layouts: 15.4 us -> none  [the longest x1 15.3 us: per_device(): outgoing = outgoing.reshape(dest_count, slot_count, block_size, rank_cols)]
  transfers between devices with their start and end apart: 2 -> 0, of which waited for: 1 -> 0; matrix products, arithmetic and copies ran while one was open for 22% -> 0% of each run, Pallas kernels for 0% -> 0%
where the time goes in v1:
time: 95.6 us; the launch traced here: 95.3 us
  Pallas kernels  86.8 us (91%)
  local copies, waits for them, and re-layouts  4.76 us (5%)
  other arithmetic  3.05 us (3%)
    pallas_call x1, Pallas kernels, reduced(): pl.pallas_call(reduce_kernel, out_shape=(jax.ShapeDtypeStruct((256, BS),...  77.9 us
    pallas_call x1, Pallas kernels, factored(): pl.pallas_call(factor_kernel, out_shape=(jax.ShapeDtypeStruct((512, RANK)...  8.89 us
    unnamed x5, local copies, waits for them, and re-layouts  3.98 us

profile of v1, /device:TPU:0, one launch (start us, length us, event | category | flops | bytes accessed | tf_op | source)
XLA Modules:
  0.0 95.3 jit_solution(439907318795303208)
XLA Ops:
  0.6 0.9 select_reduce_fusion.1
  1.6 0.8 select_reduce_fusion
  2.4 1.3 %pad_add_fusion.refs_0_ = s32[1024]{0:T(1024)} fusion(s32[512]{0:T(512)S(1)} %compare_select_fusion, s32[256]{0:T(256)S(1)} %compare_select_fusion.1, s32[256]{0:T(256)} %param.7), kind=kLoop, calls=%fused_computation.6 | loop fusion | flops 2048 | bytes 8192 | tf_op jit(solution)/shard_map/concatenate | solution.py:395
  3.7 2.4 %copy.8.refs_1_ = f32[2048,64]{1,0:T(8,128)} copy(f32[2048,64]{0,1:T(8,128)} %param.5) | data formatting | bytes 1048576 | tf_op args[1]
  6.1 77.9 %reduce.1 = (f32[256,128]{1,0:T(8,128)}, f32[32,128]{1,0:T(8,128)}) custom-call(s32[1024]{0:T(1024)} %pad_add_fusion.refs_0_, f32[2048,64]{1,0:T(8,128)} %copy.8.refs_1_, f32[256,128,128]{2,1,0:T(8,128)} %refs_2_.1), custom_call_target="tpu_custom_call" | custom-call | tf_op jit(solution)/shard_map/reduce/pallas_call | solution.py:360
  84.0 0.0 copy-start
  84.0 0.9 copy-done
  84.9 0.0 copy-start.1
  84.9 0.7 copy-done.1
  85.6 8.9 %factor.1 = (f32[512,64]{1,0:T(8,128)S(1)}, f32[64,64]{1,0:T(8,128)}) custom-call(f32[32,128]{1,0:T(8,128)S(1)} %copy-done.1, f32[256,128]{1,0:T(8,128)S(1)} %copy-done), custom_call_target="tpu_custom_call" | custom-call | tf_op jit(solution)/shard_map/factor/pallas_call | solution.py:377
  94.5 0.8 copy.9
  (2 shorter events, 0.0 us)
Async XLA Ops:
  84.0 0.9 copy-start
  84.9 0.7 copy-start.1

commit v2 on v1

v2 whole, which is shorter than its diff:
```python
import functools

import jax
import jax.numpy as jnp
from jax import lax
from jax.experimental import pallas as pl
from jax.experimental.pallas import tpu as pltpu
from jax.sharding import PartitionSpec as P

MESH = pl.DeviceIdType.MESH
F32 = jnp.float32
BF16 = jnp.bfloat16
NB = 256
BS = 128
RANK = 64
ROWS = 4
NRB = 512
HALF = BS // 2
PK = HALF // 2
CHUNKS = 4
PER = NB // CHUNKS
NCOL = 16
AXES = ("x", "y", "z")
STRIDE = {"x": 1, "z": 4, "y": 32}
FLOWS = (
    (0, 0, 6, "xyz"),
    (0, 6, 11, "yzx"),
    (0, 11, 16, "zxy"),
    (1, 0, 5, "xyz"),
    (1, 5, 11, "yzx"),
    (1, 11, 16, "zxy"),
)
NF = len(FLOWS)
ORDER = (2, 3, 1, 0)
SPLITS = (((0, 2), (2, 4)), ((0, 4),), ((0, 1), (1, 2), (2, 3), (3, 4)))


def coords():
    g, d = lax.axis_index("grp"), lax.axis_index("dev")
    return {"x": d % 4, "z": d // 4, "y": g // 2, "c": g % 2}


def device(me, **moved):
    at = dict(me)
    at.update(moved)
    return (at["y"] * 2 + at["c"], at["z"] * 4 + at["x"])


def neighbour(me, axis, step):
    return device(me, **{axis: (me[axis] + step + 4) % 4})


def groups_of(first, end):
    out, tile = [], first
    while tile < end:
        row, within = divmod(tile, 4)
        count = min(4 - within, end - tile)
        out.append((row, within, count, tile - first))
        tile += count
    return out


def remote(src, dst, send, recv, to):
    return pltpu.make_async_remote_copy(
        src_ref=src, dst_ref=dst, send_sem=send, recv_sem=recv, device_id=to, device_id_type=MESH
    )


def reduce_kernel(*refs):
    cols, rows_in, panel_t, blocks, out_ref = refs[:5]
    refs = list(refs[5:])
    held, weights, sums, panel, table, meta = refs[:6]
    refs = refs[6:]
    mine_out, pair_in, a1, b1, b2, s1, a2, b12, b22, q2, c3 = (
        refs[NF * i : NF * (i + 1)] for i in range(11)
    )
    (gbuf, aux_sem, hbm_sem, pair_s, pair_r, one_s, one_r, two_s, two_r, three_s, three_r, gram_s, gram_r) = refs[NF * 11 :]
    me = coords()

    panel_copy = pltpu.make_async_copy(panel_t, panel, aux_sem.at[0])
    panel_copy.start()

    def load(half, c):
        part = (pl.ds(c * PER, PER), pl.ds(half * HALF, HALF))
        return pltpu.make_async_copy(blocks.at[part], held.at[part], hbm_sem.at[half, c])

    for c in range(2):
        load(0, c).start()

    barrier = pltpu.get_barrier_semaphore()
    peers = [device(me, c=1 - me["c"])]
    for axis in AXES:
        peers += [neighbour(me, axis, step) for step in (1, 2, 3)]
    for peer in peers:
        pl.semaphore_signal(barrier, inc=1, device_id=peer, device_id_type=MESH)

    lane = lax.broadcasted_iota(jnp.int32, (BS, BS), 1)
    sub = lax.broadcasted_iota(jnp.int32, (BS, BS), 0)
    across = [jnp.broadcast_to(rows_in[:, i * BS : (i + 1) * BS].astype(F32), (BS, BS)) for i in range(2)]
    down = [x.T for x in across]
    for i in range(2):
        best = jnp.full((1, BS), -1, jnp.int32)
        for q in range(i + 1):
            same = across[i] == down[q]
            if q == i:
                same = same & (sub < lane)
            best = jnp.maximum(best, jnp.max(jnp.where(same, sub + q * BS, -1), axis=0, keepdims=True))
        table[:, i * BS : (i + 1) * BS] = jnp.where(best < 0, NB, best)
    for i in range(NRB // BS):
        best = jnp.full((1, BS), -1, jnp.int32)
        target = (lane + i * BS).astype(F32)
        for q in range(2):
            best = jnp.maximum(best, jnp.max(jnp.where(target == down[q], sub + q * BS, -1), axis=0, keepdims=True))
        table[:, NB + i * BS : NB + (i + 1) * BS] = jnp.where(best < 0, NB, best)
    table_copy = pltpu.make_async_copy(table, meta, aux_sem.at[1])
    table_copy.start()

    lane_low = lax.broadcasted_iota(jnp.int32, (PK, BS), 1) < RANK
    panel_copy.wait()

    for c in range(NCOL):
        p = panel[:, c * BS : (c + 1) * BS]
        high = p.astype(BF16).astype(F32)
        both = jnp.concatenate([high, p - high], axis=0).T.astype(BF16)
        weights[c, :BS, :] = both
        weights[c, BS:, :] = both
    for half in range(2):
        sums[half, NB] = jnp.zeros((PK, BS), F32)
    table_copy.wait()

    def multiply(half):
        def step(c, _):
            load(half, c).wait()
            if half == 0:
                ahead = c + 2
                load(ahead // CHUNKS, ahead % CHUNKS).start()
            out = []
            for i in range(PER):
                k = c * PER + i
                x = held[k, half * HALF : (half + 1) * HALF, :]
                high = x.astype(BF16)
                low = (x - high.astype(F32)).astype(BF16)
                left = jnp.concatenate([high, low], axis=1)
                u = jnp.dot(left, weights[cols[k]], preferred_element_type=F32)
                top, bottom = u[:PK], u[PK:]
                out.append(
                    jnp.where(lane_low, top, bottom)
                    + pltpu.roll(jnp.where(lane_low, bottom, top), RANK, 1)
                )
            for i in range(PER):
                k = c * PER + i
                sums[half, k] = out[i] + sums[half, meta[0, k]]
            return 0

        lax.fori_loop(0, CHUNKS, step, 0)

    def owner(f, core, ua, ub, uc):
        half, _, _, order = FLOWS[f]
        sign = 1 if half == 0 else -1
        at = core * 16
        for axis, u in zip(order, (ua, ub, uc)):
            at = at + STRIDE[axis] * ((me[axis] + (sign * u) % 4) % 4)
        return at

    def own_rows(f, core, ua, ub, uc):
        half, first, end, _ = FLOWS[f]
        o = owner(f, core, ua, ub, uc)
        for row, within, count, offset in groups_of(first, end):
            at = meta[0, NB + o * ROWS + row]
            yield offset, count, sums[half, at, within * 8 : (within + count) * 8, :]

    def neigh(f, order_at, direction):
        half, _, _, order = FLOWS[f]
        sign = 1 if half == 0 else -1
        return neighbour(me, order[order_at], sign * direction)

    started = []

    def go(copy):
        copy.start()
        started.append(copy)
        return copy

    def pair_copy(f, ua):
        return remote(
            mine_out[f].at[ua], pair_in[f].at[ua], pair_s.at[f, ua], pair_r.at[f, ua], device(me, c=1 - me["c"])
        )

    def fill(f, ua):
        for pb in range(4):
            for pc in range(4):
                for offset, count, value in own_rows(f, 1 - me["c"], ua, ORDER[pb], ORDER[pc]):
                    mine_out[f][ua, pb, pc, offset * 8 : (offset + count) * 8, :] = value
        return go(pair_copy(f, ua))

    def one_copy(f, kind, part):
        ua, buf, direction = ((2, a1, 1), (3, b1, -1), (1, b2, 1))[kind]
        lo, hi = SPLITS[kind][part]
        at = pl.ds(lo, hi - lo)
        return remote(
            pair_in[f].at[ua, at], buf[f].at[at], one_s.at[f, kind, part], one_r.at[f, kind, part], neigh(f, 0, direction)
        )

    def chip_sum(f, ua, pb, extra, out):
        for pc in range(4):
            for offset, count, value in own_rows(f, me["c"], ua, ORDER[pb], ORDER[pc]):
                rows = slice(offset * 8, (offset + count) * 8)
                value = value + pair_in[f][ua, pb, pc, rows, :]
                for e in extra:
                    value = value + e[f][pb, pc, rows, :]
                out[pc, rows, :] = value

    def begin(flows):
        pairs = {}
        for ua in ORDER:
            for f in flows:
                pairs[f, ua] = fill(f, ua)
        for kind, ua in ((0, 2), (1, 3)):
            for f in flows:
                pairs[f, ua].wait_recv()
                for part, (lo, hi) in enumerate(SPLITS[kind]):
                    for pb in range(lo, hi):
                        chip_sum(f, ua, pb, (), pair_in[f].at[ua, pb])
                    go(one_copy(f, kind, part))
        return pairs

    multiply(0)
    for c in range(2, CHUNKS):
        load(1, c).start()
    pl.semaphore_wait(barrier, len(peers))
    pairs = begin((0, 1, 2))
    multiply(1)
    pairs.update(begin((3, 4, 5)))

    for part in range(4):
        for f in range(NF):
            if part == 0:
                pairs[f, 1].wait_recv()
            if part % 2 == 0:
                one_copy(f, 0, part // 2).wait_recv()
            chip_sum(f, 1, part, (a1,), pair_in[f].at[1, part])
            go(one_copy(f, 2, part))

    def two_copy(f, kind):
        pb, buf, direction = ((0, a2, 1), (1, b12, -1), (2, b22, 1))[kind]
        return remote(s1[f].at[pb], buf[f], two_s.at[f, kind], two_r.at[f, kind], neigh(f, 1, direction))

    def three_copy(f, pc):
        return remote(q2[f].at[pc], c3[f].at[pc], three_s.at[f, pc], three_r.at[f, pc], neigh(f, 2, ORDER[pc]))

    for part in range(4):
        for f in range(NF):
            if part == 0:
                pairs[f, 0].wait_recv()
                one_copy(f, 1, 0).wait_recv()
            one_copy(f, 2, part).wait_recv()
            chip_sum(f, 0, part, (b1, b2), s1[f].at[part])
            if part < 2:
                go(two_copy(f, part))
            elif part == 2:
                two_copy(f, 0).wait_recv()
                s1[f][2] = s1[f][2] + a2[f][...]
                go(two_copy(f, 2))
    for f in range(NF):
        two_copy(f, 1).wait_recv()
        two_copy(f, 2).wait_recv()
        q2[f][...] = s1[f][3] + b12[f][...] + b22[f][...]
        for pc in range(3):
            go(three_copy(f, pc))
    for f in range(NF):
        half, first, end, _ = FLOWS[f]
        for pc in range(3):
            three_copy(f, pc).wait_recv()
        out_ref[half * 128 + first * 8 : half * 128 + end * 8, :] = (
            q2[f][3] + c3[f][0] + (c3[f][1] + c3[f][2])
        )

    prod = out_ref[:256, :]
    both = lax.dot_general(
        prod, prod, (((0,), (0,)), ((), ())), precision=lax.Precision.HIGHEST, preferred_element_type=F32
    )
    upper, lower = both[:RANK], both[RANK:]
    in_low = upper + pltpu.roll(lower, RANK, 1)
    in_high = pltpu.roll(upper, RANK, 1) + lower
    gbuf[0, 0] = jnp.where(lane_low, in_low[:PK], in_high[PK:]) * (1.0 / (NRB * BS))

    copy = go(remote(gbuf.at[0, 0], gbuf.at[0, 1], gram_s.at[0, 0], gram_r.at[0, 0], device(me, c=1 - me["c"])))
    copy.wait_recv()
    total = gbuf[0, 0] + gbuf[0, 1]
    for i, axis in enumerate(AXES):
        gbuf[i + 1, 0] = total
        copies = [
            go(
                remote(
                    gbuf.at[i + 1, 0],
                    gbuf.at[i + 1, step],
                    gram_s.at[i + 1, step - 1],
                    gram_r.at[i + 1, step - 1],
                    neighbour(me, axis, step),
                )
            )
            for step in (1, 2, 3)
        ]
        for copy in copies:
            copy.wait_recv()
        total = (gbuf[i + 1, 0] + gbuf[i + 1, 2]) + (gbuf[i + 1, 1] + gbuf[i + 1, 3])
    out_ref[256:, :] = total
    for copy in started:
        copy.wait_send()


def factor_kernel(in_ref, basis_ref, r_ref):
    lane = lax.broadcasted_iota(jnp.int32, (8, BS), 1)
    sub = lax.broadcasted_iota(jnp.int32, (8, BS), 0)
    packed = in_ref[256:, :]
    turned = pltpu.roll(packed, RANK, 1)
    tiles = []
    for t in range(8):
        half = packed if t < 4 else turned
        g = half[(t % 4) * 8 : (t % 4 + 1) * 8, :]
        eye = (lane - RANK == sub + t * 8).astype(F32)
        tiles.append(jnp.where(lane < RANK, g, eye))

    def row_of(x, j):
        return jnp.broadcast_to(x[j : j + 1, :], (8, BS))

    def column_of(x, j):
        return jnp.broadcast_to(x[:, j : j + 1], (8, BS))

    done = []
    for t in range(8):
        cols = [column_of(tiles[t], 8 * t + j) for j in range(8)]
        rest = {u: [column_of(tiles[u], 8 * t + j) for j in range(8)] for u in range(t + 1, 8)}
        forward = full = tiles[t]
        pivots = inverses = jnp.ones((8, BS), F32)
        for j in range(8):
            pivot = row_of(cols[j], j)
            inverse = 1.0 / pivot
            pivots = jnp.where(sub == j, pivot, pivots)
            inverses = jnp.where(sub == j, inverse, inverses)
            c = cols[j] * inverse
            others = jnp.where(sub == j, 0.0, c)
            for k in range(j + 1, 8):
                cols[k] = cols[k] - others * row_of(cols[k], j)
            row = row_of(full, j)
            forward = forward - jnp.where(sub > j, c, 0.0) * row
            full = full - others * row
        full = full * inverses
        rows = [row_of(full, j) for j in range(8)]
        for u in range(t + 1, 8):
            p = [rest[u][j] * rows[j] for j in range(8)]
            p = [p[0] + p[1], p[2] + p[3], p[4] + p[5], p[6] + p[7]]
            tiles[u] = tiles[u] - ((p[0] + p[1]) + (p[2] + p[3]))
        scale = lax.rsqrt(pivots)
        done.append(forward * (scale * (1.5 - 0.5 * pivots * scale * scale)))
    scaled = jnp.concatenate(done, axis=0)
    lane = lax.broadcasted_iota(jnp.int32, (RANK, BS), 1)
    sub = lax.broadcasted_iota(jnp.int32, (RANK, BS), 0)
    r_ref[...] = jnp.where(lane >= sub, scaled, 0.0)[:, :RANK]
    inverse = pltpu.roll(jnp.where(lane >= RANK, scaled, 0.0), RANK, 1)
    prod = in_ref[:256, :]
    turned = pltpu.roll(prod, RANK, 1)
    for r in range(ROWS):
        part = jnp.concatenate(
            [x[half * BS + r * PK : half * BS + (r + 1) * PK] for half in range(2) for x in (prod, turned)], axis=0
        )
        basis_ref[:, r * BS : (r + 1) * BS] = lax.dot_general(
            inverse, part, (((1,), (1,)), ((), ())), precision=lax.Precision.HIGHEST, preferred_element_type=F32
        )


def reduced(cols, rows_in, panel_t, blocks):
    rows = [(end - first) * 8 for _, first, end, _ in FLOWS]

    def per_flow(*lead):
        return [pltpu.VMEM((*lead, n, BS), F32) for n in rows]

    dma = pltpu.SemaphoreType.DMA
    scratch = [
        pltpu.VMEM((NB, BS, BS), F32),
        pltpu.VMEM((16, 2 * BS, BS), BF16),
        pltpu.VMEM((2, NB + 1, PK, BS), F32),
        pltpu.VMEM((RANK, NCOL * BS), F32),
        pltpu.VMEM((1, NB + NRB), jnp.int32),
        pltpu.SMEM((1, NB + NRB), jnp.int32),
        *per_flow(4, 4, 4),
        *per_flow(4, 4, 4),
        *per_flow(4, 4),
        *per_flow(4, 4),
        *per_flow(4, 4),
        *per_flow(4, 4),
        *per_flow(4),
        *per_flow(4),
        *per_flow(4),
        *per_flow(4),
        *per_flow(3),
        pltpu.VMEM((4, 4, PK, BS), F32),
        dma((2,)),
        dma((2, CHUNKS)),
        dma((NF, 4)),
        dma((NF, 4)),
        dma((NF, 3, 4)),
        dma((NF, 3, 4)),
        dma((NF, 3)),
        dma((NF, 3)),
        dma((NF, 3)),
        dma((NF, 3)),
        dma((4, 3)),
        dma((4, 3)),
    ]
    return pl.pallas_call(
        reduce_kernel,
        out_shape=jax.ShapeDtypeStruct((256 + PK, BS), F32),
        in_specs=[
            pl.BlockSpec(memory_space=pltpu.SMEM),
            pl.BlockSpec(memory_space=pltpu.VMEM),
            pl.BlockSpec(memory_space=pl.ANY),
            pl.BlockSpec(memory_space=pl.ANY),
        ],
        out_specs=pl.BlockSpec(memory_space=pltpu.VMEM),
        scratch_shapes=scratch,
        compiler_params=pltpu.CompilerParams(collective_id=0, has_side_effects=True, vmem_limit_bytes=60 << 20),
        name="reduce",
    )(cols, rows_in, panel_t, blocks)


def factored(result):
    vmem = pl.BlockSpec(memory_space=pltpu.VMEM)
    return pl.pallas_call(
        factor_kernel,
        out_shape=(jax.ShapeDtypeStruct((RANK, 512), F32), jax.ShapeDtypeStruct((RANK, RANK), F32)),
        in_specs=[vmem],
        out_specs=(vmem, vmem),
        compiler_params=pltpu.CompilerParams(vmem_limit_bytes=16 << 20),
        name="factor",
    )(result)


def per_device(blocks, panel, block_rows, block_cols):
    result = reduced(block_cols, block_rows.reshape(1, NB), panel.T, blocks)
    basis_t, r = factored(result)
    return basis_t.T, r


def solution(mesh):
    placed = (
        P(("grp", "dev"), None, None),
        P(("grp", "dev"), None),
        P(("grp", "dev")),
        P(("grp", "dev")),
    )
    return jax.shard_map(
        per_device,
        mesh=mesh,
        in_specs=placed,
        out_specs=(P(("grp", "dev"), None), P()),
        check_vma=False,
    )
```

time: 95.6 us -> 70.7 us (0.74)
  Pallas kernels: 86.8 us -> 69 us
  local copies, waits for them, and re-layouts: 4.76 us -> 0.9 us
  other arithmetic: 3.05 us -> 0 us
    pallas_call x2, Pallas kernels: 86.8 us -> 69 us  [the longest x1 65.7 us: reduced(): pl.pallas_call(reduce_kernel, out_shape=jax.ShapeDtypeStruct((256 + PK, B...]
    unnamed x5 -> x2, local copies, waits for them, and re-layouts: 3.98 us -> 0.9 us
    reduce_max x2 -> x0, other arithmetic: 1.76 us -> none  [the longest x1 0.93 us: per_device(): previous = jnp.max(jnp.where(same, k[None, :], -1), axis=1)]
    concatenate x1 -> x0, other arithmetic: 1.28 us -> none  [per_device(): meta = jnp.concatenate([block_cols, previous, last])]
where the time goes in v2:
time: 70.7 us; the launch traced here: 70.6 us
  Pallas kernels  69 us (98%)
  local copies, waits for them, and re-layouts  0.9 us (1%)
    pallas_call x1, Pallas kernels, reduced(): pl.pallas_call(reduce_kernel, out_shape=jax.ShapeDtypeStruct((256 + PK, B...  65.7 us
    pallas_call x1, Pallas kernels, factored(): pl.pallas_call(factor_kernel, out_shape=(jax.ShapeDtypeStruct((RANK, 512)...  3.31 us

profile of v2, /device:TPU:0, one launch (start us, length us, event | category | flops | bytes accessed | tf_op | source)
XLA Modules:
  0.0 70.6 jit_solution(3160254908566966899)
XLA Ops:
  0.6 65.7 %reduce.1.in_ref = f32[288,128]{1,0:T(8,128)} custom-call(s32[256]{0:T(256)} %refs_0_.1, s32[1,256]{1,0:T(1,128)} %bitcast.4, f32[64,2048]{1,0:T(8,128)} %bitcast.3, f32[256,128,128]{2,1,0:T(8,128)} %refs_3_.1), custom_call_target="tpu_custom_call" | custom-call | tf_op jit(solution)/shard_map/reduce/pallas_call | solution.py:411
  66.4 0.0 copy-start
  66.4 0.9 %copy-done = f32[288,128]{1,0:T(8,128)S(1)} copy-done((f32[288,128]{1,0:T(8,128)S(1)}, f32[288,128]{1,0:T(8,128)}, u32[]{:S(2)}) %copy-start) | copy-done | bytes 147480
  67.3 3.3 %factor.1 = (f32[64,512]{1,0:T(8,128)}, f32[64,64]{1,0:T(8,128)}) custom-call(f32[288,128]{1,0:T(8,128)S(1)} %copy-done), custom_call_target="tpu_custom_call" | custom-call | tf_op jit(solution)/shard_map/factor/pallas_call | solution.py:429
Async XLA Ops:
  66.4 0.9 %copy-start = (f32[288,128]{1,0:T(8,128)S(1)}, f32[288,128]{1,0:T(8,128)}, u32[]{:S(2)}) copy-start(f32[288,128]{1,0:T(8,128)} %reduce.1.in_ref) | copy-start | bytes 442372

commit v3 on v2

--- a/solution.py
+++ b/solution.py
@@ -32,7 +32,7 @@
 )
 NF = len(FLOWS)
 ORDER = (2, 3, 1, 0)
-SPLITS = (((0, 2), (2, 4)), ((0, 4),), ((0, 1), (1, 2), (2, 3), (3, 4)))
+SPLITS = (((0, 2), (2, 4)), ((0, 2), (2, 4)), ((0, 1), (1, 2), (2, 3), (3, 4)))
 
 
 def coords():
@@ -67,18 +67,22 @@
 
 
 def reduce_kernel(*refs):
-    cols, rows_in, panel_t, blocks, out_ref = refs[:5]
+    cols_in, rows_at, panel_t, blocks, out_ref = refs[:5]
     refs = list(refs[5:])
-    held, weights, sums, panel, table, meta = refs[:6]
-    refs = refs[6:]
+    held, weights, sums, panel, table, meta, cols, rows_in = refs[:8]
+    refs = refs[8:]
     mine_out, pair_in, a1, b1, b2, s1, a2, b12, b22, q2, c3 = (
         refs[NF * i : NF * (i + 1)] for i in range(11)
     )
     (gbuf, aux_sem, hbm_sem, pair_s, pair_r, one_s, one_r, two_s, two_r, three_s, three_r, gram_s, gram_r) = refs[NF * 11 :]
     me = coords()
 
+    rows_copy = pltpu.make_async_copy(rows_at, rows_in, aux_sem.at[2])
+    rows_copy.start()
     panel_copy = pltpu.make_async_copy(panel_t, panel, aux_sem.at[0])
     panel_copy.start()
+    cols_copy = pltpu.make_async_copy(cols_in, cols, aux_sem.at[3])
+    cols_copy.start()
 
     def load(half, c):
         part = (pl.ds(c * PER, PER), pl.ds(half * HALF, HALF))
@@ -94,6 +98,7 @@
     for peer in peers:
         pl.semaphore_signal(barrier, inc=1, device_id=peer, device_id_type=MESH)
 
+    rows_copy.wait()
     lane = lax.broadcasted_iota(jnp.int32, (BS, BS), 1)
     sub = lax.broadcasted_iota(jnp.int32, (BS, BS), 0)
     across = [jnp.broadcast_to(rows_in[:, i * BS : (i + 1) * BS].astype(F32), (BS, BS)) for i in range(2)]
@@ -127,6 +132,7 @@
     for half in range(2):
         sums[half, NB] = jnp.zeros((PK, BS), F32)
     table_copy.wait()
+    cols_copy.wait()
 
     def multiply(half):
         def step(c, _):
@@ -181,17 +187,22 @@
         started.append(copy)
         return copy
 
-    def pair_copy(f, ua):
+    def pair_copy(f, ua, piece):
+        at = pl.ds(piece * 2, 2)
         return remote(
-            mine_out[f].at[ua], pair_in[f].at[ua], pair_s.at[f, ua], pair_r.at[f, ua], device(me, c=1 - me["c"])
+            mine_out[f].at[ua, at],
+            pair_in[f].at[ua, at],
+            pair_s.at[f, ua, piece],
+            pair_r.at[f, ua, piece],
+            device(me, c=1 - me["c"]),
         )
 
-    def fill(f, ua):
-        for pb in range(4):
+    def fill(f, ua, piece):
+        for pb in (piece * 2, piece * 2 + 1):
             for pc in range(4):
                 for offset, count, value in own_rows(f, 1 - me["c"], ua, ORDER[pb], ORDER[pc]):
                     mine_out[f][ua, pb, pc, offset * 8 : (offset + count) * 8, :] = value
-        return go(pair_copy(f, ua))
+        go(pair_copy(f, ua, piece))
 
     def one_copy(f, kind, part):
         ua, buf, direction = ((2, a1, 1), (3, b1, -1), (1, b2, 1))[kind]
@@ -211,32 +222,29 @@
                 out[pc, rows, :] = value
 
     def begin(flows):
-        pairs = {}
-        for ua in ORDER:
+        for ua, piece in ((2, 0), (3, 0), (2, 1), (3, 1), (1, 0), (1, 1), (0, 0), (0, 1)):
             for f in flows:
-                pairs[f, ua] = fill(f, ua)
-        for kind, ua in ((0, 2), (1, 3)):
-            for f in flows:
-                pairs[f, ua].wait_recv()
-                for part, (lo, hi) in enumerate(SPLITS[kind]):
-                    for pb in range(lo, hi):
+                fill(f, ua, piece)
+        for part in (0, 1):
+            for kind, ua in ((0, 2), (1, 3)):
+                for f in flows:
+                    pair_copy(f, ua, part).wait_recv()
+                    for pb in range(*SPLITS[kind][part]):
                         chip_sum(f, ua, pb, (), pair_in[f].at[ua, pb])
                     go(one_copy(f, kind, part))
-        return pairs
 
     multiply(0)
     for c in range(2, CHUNKS):
         load(1, c).start()
     pl.semaphore_wait(barrier, len(peers))
-    pairs = begin((0, 1, 2))
+    begin((0, 1, 2))
     multiply(1)
-    pairs.update(begin((3, 4, 5)))
+    begin((3, 4, 5))
 
     for part in range(4):
         for f in range(NF):
-            if part == 0:
-                pairs[f, 1].wait_recv()
             if part % 2 == 0:
+                pair_copy(f, 1, part // 2).wait_recv()
                 one_copy(f, 0, part // 2).wait_recv()
             chip_sum(f, 1, part, (a1,), pair_in[f].at[1, part])
             go(one_copy(f, 2, part))
@@ -250,9 +258,9 @@
 
     for part in range(4):
         for f in range(NF):
-            if part == 0:
-                pairs[f, 0].wait_recv()
-                one_copy(f, 1, 0).wait_recv()
+            if part % 2 == 0:
+                pair_copy(f, 0, part // 2).wait_recv()
+                one_copy(f, 1, part // 2).wait_recv()
             one_copy(f, 2, part).wait_recv()
             chip_sum(f, 0, part, (b1, b2), s1[f].at[part])
             if part < 2:
@@ -383,6 +391,8 @@
         pltpu.VMEM((RANK, NCOL * BS), F32),
         pltpu.VMEM((1, NB + NRB), jnp.int32),
         pltpu.SMEM((1, NB + NRB), jnp.int32),
+        pltpu.SMEM((NB,), jnp.int32),
+        pltpu.VMEM((1, NB), jnp.int32),
         *per_flow(4, 4, 4),
         *per_flow(4, 4, 4),
         *per_flow(4, 4),
@@ -395,10 +405,10 @@
         *per_flow(4),
         *per_flow(3),
         pltpu.VMEM((4, 4, PK, BS), F32),
-        dma((2,)),
+        dma((4,)),
         dma((2, CHUNKS)),
-        dma((NF, 4)),
-        dma((NF, 4)),
+        dma((NF, 4, 2)),
+        dma((NF, 4, 2)),
         dma((NF, 3, 4)),
         dma((NF, 3, 4)),
         dma((NF, 3)),
@@ -412,8 +422,8 @@
         reduce_kernel,
         out_shape=jax.ShapeDtypeStruct((256 + PK, BS), F32),
         in_specs=[
-            pl.BlockSpec(memory_space=pltpu.SMEM),
-            pl.BlockSpec(memory_space=pltpu.VMEM),
+            pl.BlockSpec(memory_space=pl.ANY),
+            pl.BlockSpec(memory_space=pl.ANY),
             pl.BlockSpec(memory_space=pl.ANY),
             pl.BlockSpec(memory_space=pl.ANY),
         ],

time: 70.7 us -> 69.1 us (0.977)
  Pallas kernels: 69 us -> 67.4 us
    pallas_call x1, Pallas kernels: 65.7 us -> 64.1 us  [reduced(): pl.pallas_call(reduce_kernel, out_shape=jax.ShapeDtypeStruct((256 + PK, B...]
where the time goes in v3:
time: 69.1 us; the launch traced here: 68.9 us
  Pallas kernels  67.4 us (98%)
  local copies, waits for them, and re-layouts  0.9 us (1%)
    pallas_call x1, Pallas kernels, reduced(): pl.pallas_call(reduce_kernel, out_shape=jax.ShapeDtypeStruct((256 + PK, B...  64.1 us
    pallas_call x1, Pallas kernels, factored(): pl.pallas_call(factor_kernel, out_shape=(jax.ShapeDtypeStruct((RANK, 512)...  3.31 us

profile of v3, /device:TPU:0, one launch (start us, length us, event | category | flops | bytes accessed | tf_op | source)
XLA Modules:
  0.0 68.9 jit_solution(17709981800210975331)
XLA Ops:
  0.6 64.1 %reduce.1.in_ref = f32[288,128]{1,0:T(8,128)} custom-call(s32[256]{0:T(256)} %refs_0_.1, s32[1,256]{1,0:T(1,128)} %bitcast.4, f32[64,2048]{1,0:T(8,128)} %bitcast.3, f32[256,128,128]{2,1,0:T(8,128)} %refs_3_.1), custom_call_target="tpu_custom_call" | custom-call | tf_op jit(solution)/shard_map/reduce/pallas_call | solution.py:421
  64.7 0.0 copy-start
  64.7 0.9 %copy-done = f32[288,128]{1,0:T(8,128)S(1)} copy-done((f32[288,128]{1,0:T(8,128)S(1)}, f32[288,128]{1,0:T(8,128)}, u32[]{:S(2)}) %copy-start) | copy-done | bytes 147480
  65.6 3.3 %factor.1 = (f32[64,512]{1,0:T(8,128)}, f32[64,64]{1,0:T(8,128)}) custom-call(f32[288,128]{1,0:T(8,128)S(1)} %copy-done), custom_call_target="tpu_custom_call" | custom-call | tf_op jit(solution)/shard_map/factor/pallas_call | solution.py:439
Async XLA Ops:
  64.7 0.9 %copy-start = (f32[288,128]{1,0:T(8,128)S(1)}, f32[288,128]{1,0:T(8,128)}, u32[]{:S(2)}) copy-start(f32[288,128]{1,0:T(8,128)} %reduce.1.in_ref) | copy-start | bytes 442372

commit v4 on v3

--- a/solution.py
+++ b/solution.py
@@ -317,10 +317,15 @@
         copy.wait_send()
 
 
-def factor_kernel(in_ref, basis_ref, r_ref):
+def factor_kernel(in_ref, basis_ref, r_ref, gram, prod_in, sem):
     lane = lax.broadcasted_iota(jnp.int32, (8, BS), 1)
     sub = lax.broadcasted_iota(jnp.int32, (8, BS), 0)
-    packed = in_ref[256:, :]
+    gram_copy = pltpu.make_async_copy(in_ref.at[pl.ds(256, PK)], gram, sem.at[0])
+    gram_copy.start()
+    prod_copy = pltpu.make_async_copy(in_ref.at[pl.ds(0, 256)], prod_in, sem.at[1])
+    prod_copy.start()
+    gram_copy.wait()
+    packed = gram[...]
     turned = pltpu.roll(packed, RANK, 1)
     tiles = []
     for t in range(8):
@@ -366,7 +371,8 @@
     sub = lax.broadcasted_iota(jnp.int32, (RANK, BS), 0)
     r_ref[...] = jnp.where(lane >= sub, scaled, 0.0)[:, :RANK]
     inverse = pltpu.roll(jnp.where(lane >= RANK, scaled, 0.0), RANK, 1)
-    prod = in_ref[:256, :]
+    prod_copy.wait()
+    prod = prod_in[...]
     turned = pltpu.roll(prod, RANK, 1)
     for r in range(ROWS):
         part = jnp.concatenate(
@@ -439,9 +445,10 @@
     return pl.pallas_call(
         factor_kernel,
         out_shape=(jax.ShapeDtypeStruct((RANK, 512), F32), jax.ShapeDtypeStruct((RANK, RANK), F32)),
-        in_specs=[vmem],
+        in_specs=[pl.BlockSpec(memory_space=pl.ANY)],
         out_specs=(vmem, vmem),
-        compiler_params=pltpu.CompilerParams(vmem_limit_bytes=16 << 20),
+        scratch_shapes=[pltpu.VMEM((PK, BS), F32), pltpu.VMEM((256, BS), F32), pltpu.SemaphoreType.DMA((2,))],
+        compiler_params=pltpu.CompilerParams(vmem_limit_bytes=60 << 20),
         name="factor",
     )(result)
 

time: 69.1 us -> 69.1 us (level)
  local copies, waits for them, and re-layouts: 0.9 us -> 0 us
  Pallas kernels: 67.4 us -> 68.2 us
    unnamed x2 -> x0, local copies, waits for them, and re-layouts: 0.9 us -> none
    pallas_call x1, Pallas kernels: 3.31 us -> 4.17 us  [factored(): pl.pallas_call(factor_kernel, out_shape=(jax.ShapeDtypeStruct((RANK, 512)...]
where the time goes in v4:
time: 69.1 us; the launch traced here: 68.9 us
  Pallas kernels  68.2 us (99%)
    pallas_call x1, Pallas kernels, reduced(): pl.pallas_call(reduce_kernel, out_shape=jax.ShapeDtypeStruct((256 + PK, B...  64.1 us
    pallas_call x1, Pallas kernels, factored(): pl.pallas_call(factor_kernel, out_shape=(jax.ShapeDtypeStruct((RANK, 512)...  4.17 us

profile of v4, /device:TPU:0, one launch (start us, length us, event | category | flops | bytes accessed | tf_op | source)
XLA Modules:
  0.0 68.9 jit_solution(14412879130397005995)
XLA Ops:
  0.6 64.1 %reduce.1.in_ref = f32[288,128]{1,0:T(8,128)} custom-call(s32[256]{0:T(256)} %refs_0_.1, s32[1,256]{1,0:T(1,128)} %bitcast.4, f32[64,2048]{1,0:T(8,128)} %bitcast.3, f32[256,128,128]{2,1,0:T(8,128)} %refs_3_.1), custom_call_target="tpu_custom_call" | custom-call | tf_op jit(solution)/shard_map/reduce/pallas_call | solution.py:427
  64.7 4.2 %factor.1 = (f32[64,512]{1,0:T(8,128)}, f32[64,64]{1,0:T(8,128)}) custom-call(f32[288,128]{1,0:T(8,128)} %reduce.1.in_ref), custom_call_target="tpu_custom_call" | custom-call | tf_op jit(solution)/shard_map/factor/pallas_call | solution.py:445
